TPU v7x, 256 devices: a whole 4x4x8 slice. The times are simulated.
256 devices in a mesh: dp: 32 (over y, z), seq: 8 (over x, core).
Axes of the slice: x: 4, y: 4, z: 8, core: 2. Of those that a mesh axis runs over, the one named last changes fastest.
Arguments:
- queries: bfloat16 [32, 1024, 2048], P('dp', 'seq'), may hold values from -6 to 6
- keys: bfloat16 [32, 1024, 2048], P('dp', 'seq'), may hold values from -6 to 6
- values: bfloat16 [32, 1024, 2048], P('dp', 'seq'), may hold values from -6 to 6
- grad_out: bfloat16 [32, 1024, 2048], P('dp', 'seq'), may hold values from -6 to 6
- q_gain: float32 [128], replicated, may hold values from 0.5 to 2
- k_gain: float32 [128], replicated, may hold values from 0.5 to 2
- clip_blocks: int32 [32], replicated, may hold values from 1 to 8, as said below
Outputs:
- attended: bfloat16 [32, 1024, 2048], P('dp', 'seq')
- grad_queries: bfloat16 [32, 1024, 2048], P('dp', 'seq')
- grad_keys: bfloat16 [32, 1024, 2048], P('dp', 'seq')
- grad_values: bfloat16 [32, 1024, 2048], P('dp', 'seq')
- grad_q_gain: float32 [128], replicated
- grad_k_gain: float32 [128], replicated
Inputs may be any that keep to these rules, and one draw needn't show every extreme that they name: `clip_blocks`: one clip has exactly 8 blocks; the others have at most 4.
All inputs are finite; a program needn't handle non-finite values.
Results may differ from a plain program's by a relative error of at most 0.011.
Values may be sent and summed in bfloat16 or wider, within the bound.
A program may use at most 64 MiB of HBM per device.

v0:
```python
import functools
import math

import jax
import jax.numpy as jnp
from jax import lax
from jax.experimental import pallas as pl
from jax.experimental.pallas import tpu as pltpu
from jax.sharding import PartitionSpec as P

BLOCK = 128
NORM_EPSILON = 1e-06
MESH = pl.DeviceIdType.MESH
QROWS = 256
NT = (((1,), (1,)), ((), ()))
NN = (((1,), (0,)), ((), ()))


def dot(a, b, dims):
    return lax.dot_general(a, b, dims, preferred_element_type=jnp.float32)


def inverse_rms(x):
    return lax.rsqrt(jnp.mean(x * x, axis=-1, keepdims=True) + NORM_EPSILON)


def norm_back(x, r, gain, upstream):
    scaled = upstream * gain
    mean = jnp.mean(scaled * x, axis=-1, keepdims=True)
    grad = r * scaled - x * (r * r * r * mean)
    return grad, jnp.sum(upstream * x * r, axis=0, keepdims=True)


def kernel(sizes, heads, q_ref, k_ref, v_ref, g_ref, qg_ref, kg_ref, blocks_ref,
           o_ref, dq_ref, dk_ref, dv_ref, gain_ref,
           inb, outb, keyc, keyt, valm, valt, dk_acc, dv_acc, red_a, red_b, red_c,
           in_send, in_recv, out_send, out_recv, red_send, red_recv):
    n, ny, nz = sizes
    dp = lax.axis_index("dp")
    me = lax.axis_index("seq")
    y, z = dp // nz, lax.rem(dp, nz)
    ins = (q_ref, k_ref, g_ref, v_ref)
    outs = (o_ref, dq_ref, dk_ref, dv_ref)
    rows = q_ref.shape[1]
    total = rows * n
    width = qg_ref.shape[1]

    barrier = pltpu.get_barrier_semaphore()
    for d in range(1, n):
        pl.semaphore_signal(barrier, inc=1, device_id=(dp, lax.rem(me + d, n)), device_id_type=MESH)
    for d in range(1, ny):
        pl.semaphore_signal(barrier, inc=1, device_id=(lax.rem(y + d, ny) * nz + z, me), device_id_type=MESH)
    for d in range(1, nz):
        pl.semaphore_signal(barrier, inc=1, device_id=(y * nz + lax.rem(z + d, nz), me), device_id_type=MESH)
    pl.semaphore_wait(barrier, n + ny + nz - 3)

    my_rows = pl.ds(pl.multiple_of(me * rows, rows), rows)

    def head_columns(device, j):
        return pl.ds(pl.multiple_of((device * heads + j) * width, width), width)

    for j in range(heads):
        for a in range(4):
            pltpu.make_async_copy(
                ins[a].at[0, :, head_columns(me, j)], inb.at[a, j, my_rows, :], in_recv.at[j, a]
            ).start()

        def send(d, carry, j=j):
            peer = lax.rem(me + d, n)
            for a in range(4):
                pltpu.make_async_remote_copy(
                    src_ref=ins[a].at[0, :, head_columns(peer, j)],
                    dst_ref=inb.at[a, j, my_rows, :],
                    send_sem=in_send.at[j, a],
                    recv_sem=in_recv.at[j, a],
                    device_id=(dp, peer),
                    device_id_type=MESH,
                ).start()
            return carry

        lax.fori_loop(1, n, send, 0)

    length = blocks_ref[dp] * BLOCK
    q_gain = qg_ref[...]
    k_gain = kg_ref[...]
    scale = 1.0 / math.sqrt(width)
    key_scale = scale * math.log2(math.e)
    live_col = lax.broadcasted_iota(jnp.int32, (total, 1), 0) < length
    gain_q = jnp.zeros((1, width), jnp.float32)
    gain_k = jnp.zeros((1, width), jnp.float32)

    for j in range(heads):
        for a in range(4):
            pltpu.make_async_copy(inb.at[a, j], inb.at[a, j], in_recv.at[j, a]).wait()
        k_float = inb[1, j].astype(jnp.float32)
        k_normed = jnp.where(live_col, k_float * inverse_rms(k_float) * (k_gain * key_scale), 0.0)
        keyc[...] = k_normed.astype(jnp.bfloat16)
        keyt[...] = k_normed.T.astype(jnp.bfloat16)
        v_float = jnp.where(live_col, inb[3, j].astype(jnp.float32), 0.0)
        valm[...] = v_float.astype(jnp.bfloat16)
        valt[0:width, :] = v_float.T.astype(jnp.bfloat16)
        live_lane = lax.broadcasted_iota(jnp.int32, (16, total), 1) < length
        valt[width:, :] = jnp.where(live_lane, 1.0, 0.0).astype(jnp.bfloat16)
        dk_acc[...] = jnp.zeros_like(dk_acc)
        dv_acc[...] = jnp.zeros_like(dv_acc)

        def block(i, gain_q, j=j):
            at = pl.ds(pl.multiple_of(i * QROWS, QROWS), QROWS)
            q_float = inb[0, j, at, :].astype(jnp.float32)
            r_q = inverse_rms(q_float)
            q_half = (q_float * r_q * q_gain).astype(jnp.bfloat16)
            e = jnp.exp2(dot(keyc[...], q_half, NT))
            e_half = e.astype(jnp.bfloat16)
            out_ext = dot(valt[...], e_half, NN)
            live = i * QROWS + lax.broadcasted_iota(jnp.int32, (1, QROWS), 1) < length
            inv = jnp.where(live, 1.0 / out_ext[width:width + 1, :], 0.0)
            out_t = out_ext[0:width, :] * inv
            g_t = inb[2, j, at, :].astype(jnp.float32).T * inv
            gs = g_t.astype(jnp.bfloat16)
            row_dot = jnp.sum(g_t * out_t, axis=0, keepdims=True)
            grad_probs = dot(valm[...], gs, NN)
            ds = (e * (grad_probs - row_dot)).astype(jnp.bfloat16)
            dv_acc[...] += dot(e_half, gs, NT)
            dk_acc[...] += dot(ds, q_half, NN)
            grad_qnorm = dot(keyt[...], ds, NN).T * math.log(2.0)
            grad_q, part = norm_back(q_float, r_q, q_gain, grad_qnorm)
            outb[0, j, at, :] = out_t.T.astype(jnp.bfloat16)
            outb[1, j, at, :] = grad_q.astype(jnp.bfloat16)
            return gain_q + part

        gain_q = lax.fori_loop(0, total // QROWS, block, gain_q)
        k_float = inb[1, j].astype(jnp.float32)
        grad_knorm = jnp.where(live_col, dk_acc[...] * scale, 0.0)
        grad_k, part = norm_back(k_float, inverse_rms(k_float), k_gain, grad_knorm)
        gain_k = gain_k + part
        outb[2, j] = grad_k.astype(jnp.bfloat16)
        outb[3, j] = jnp.where(live_col, dv_acc[...], 0.0).astype(jnp.bfloat16)

        for a in range(4):
            pltpu.make_async_copy(
                outb.at[a, j, my_rows, :], outs[a].at[0, :, head_columns(me, j)], out_recv.at[a]
            ).start()

        def give(d, carry, j=j):
            peer = lax.rem(me + d, n)
            for a in range(4):
                pltpu.make_async_remote_copy(
                    src_ref=outb.at[a, j, pl.ds(pl.multiple_of(peer * rows, rows), rows), :],
                    dst_ref=outs[a].at[0, :, head_columns(me, j)],
                    send_sem=out_send.at[j, a],
                    recv_sem=out_recv.at[a],
                    device_id=(dp, peer),
                    device_id_type=MESH,
                ).start()
            return carry

        lax.fori_loop(1, n, give, 0)

    part = jnp.concatenate([gain_q, gain_k, jnp.zeros((6, width), jnp.float32)], axis=0)
    stages = (
        (red_a, n, me, lambda p: (dp, p)),
        (red_b, ny, y, lambda p: (p * nz + z, me)),
        (red_c, nz, z, lambda p: (y * nz + p, me)),
    )
    for s, (slots, count, mine, place) in enumerate(stages):
        slots[mine] = part
        copies = []
        for d in range(1, count):
            copies.append(pltpu.make_async_remote_copy(
                src_ref=slots.at[mine],
                dst_ref=slots.at[mine],
                send_sem=red_send.at[s, d],
                recv_sem=red_recv.at[s, d],
                device_id=place(lax.rem(mine + d, count)),
                device_id_type=MESH,
            ))
        for copy in copies:
            copy.start()
        for copy in copies:
            copy.wait()
        part = slots[0]
        for p in range(1, count):
            part = part + slots[p]
    gain_ref[...] = part

    for j in range(heads):
        for a in range(4):
            pltpu.make_async_copy(
                inb.at[a, j, pl.ds(0, total - rows), :], inb.at[a, j, pl.ds(0, total - rows), :], in_send.at[j, a]
            ).wait()
            pltpu.make_async_copy(
                outb.at[a, j, pl.ds(0, total - rows), :], outb.at[a, j, pl.ds(0, total - rows), :], out_send.at[j, a]
            ).wait()
    for a in range(4):
        pltpu.make_async_copy(outs[a], outs[a], out_recv.at[a]).wait()


def shards(sizes, queries, keys, values, grad_out, q_gain, k_gain, clip_blocks):
    n, ny, nz = sizes
    rows, columns = queries.shape[1:]
    width = q_gain.shape[0]
    heads = columns // width // n
    total = rows * n
    hbm = pl.BlockSpec(memory_space=pl.ANY)
    vmem = pl.BlockSpec(memory_space=pltpu.VMEM)
    wide = jax.ShapeDtypeStruct(queries.shape, jnp.bfloat16)
    half, full = jnp.bfloat16, jnp.float32
    result = pl.pallas_call(
        functools.partial(kernel, sizes, heads),
        name="attention_exchange",
        out_shape=(wide, wide, wide, wide, jax.ShapeDtypeStruct((8, width), full)),
        in_specs=[hbm, hbm, hbm, hbm, vmem, vmem, pl.BlockSpec(memory_space=pltpu.SMEM)],
        out_specs=(hbm, hbm, hbm, hbm, vmem),
        scratch_shapes=[
            pltpu.VMEM((4, heads, total, width), half),
            pltpu.VMEM((4, heads, total, width), half),
            pltpu.VMEM((total, width), half),
            pltpu.VMEM((width, total), half),
            pltpu.VMEM((total, width), half),
            pltpu.VMEM((width + 16, total), half),
            pltpu.VMEM((total, width), full),
            pltpu.VMEM((total, width), full),
            pltpu.VMEM((n, 8, width), full),
            pltpu.VMEM((ny, 8, width), full),
            pltpu.VMEM((nz, 8, width), full),
            pltpu.SemaphoreType.DMA((heads, 4)),
            pltpu.SemaphoreType.DMA((heads, 4)),
            pltpu.SemaphoreType.DMA((heads, 4)),
            pltpu.SemaphoreType.DMA((4,)),
            pltpu.SemaphoreType.DMA((3, 8)),
            pltpu.SemaphoreType.DMA((3, 8)),
        ],
        compiler_params=pltpu.CompilerParams(
            collective_id=0, has_side_effects=True, vmem_limit_bytes=48 * 2**20
        ),
    )(queries, keys, values, grad_out, q_gain.reshape(1, width), k_gain.reshape(1, width), clip_blocks)
    attended, grad_q, grad_k, grad_v, gains = result
    return attended, grad_q, grad_k, grad_v, gains[0], gains[1]


def solution(mesh):
    n = mesh.shape["seq"]
    nz = 8
    ny = mesh.shape["dp"] // nz
    placed = P("dp", "seq", None)
    return jax.shard_map(
        functools.partial(shards, (n, ny, nz)),
        mesh=mesh,
        in_specs=(placed, placed, placed, placed, P(), P(), P()),
        out_specs=(placed, placed, placed, placed, P(), P()),
        check_vma=False,
    )
```

profile of v0, /device:TPU:1, one launch (start us, length us, event | category | flops | bytes accessed | tf_op | source)
XLA Modules:
  0.0 74.6 jit_solution(10560154311415704658)
XLA Ops:
  0.6 0.0 copy-start.4
  0.6 0.0 copy-start.5
  0.7 0.0 copy-start.6
  0.7 0.6 copy-done.4
  1.3 0.0 copy-done.5
  1.3 0.0 copy-done.6
  1.3 0.0 copy-start
  1.3 1.0 %copy-done = bf16[1,128,2048]{2,1,0:T(8,128)(2,1)S(1)} copy-done((bf16[1,128,2048]{2,1,0:T(8,128)(2,1)S(1)}, bf16[1,128,2048]{2,1,0:T(8,128)(2,1)}, u32[]{:S(2)}) %copy-start) | copy-done | bytes 524312
  2.4 0.0 copy-start.1
  2.4 1.0 %copy-done.1 = bf16[1,128,2048]{2,1,0:T(8,128)(2,1)S(1)} copy-done((bf16[1,128,2048]{2,1,0:T(8,128)(2,1)S(1)}, bf16[1,128,2048]{2,1,0:T(8,128)(2,1)}, u32[]{:S(2)}) %copy-start.1) | copy-done | bytes 524312
  3.4 0.0 copy-start.2
  3.4 1.0 %copy-done.2 = bf16[1,128,2048]{2,1,0:T(8,128)(2,1)S(1)} copy-done((bf16[1,128,2048]{2,1,0:T(8,128)(2,1)S(1)}, bf16[1,128,2048]{2,1,0:T(8,128)(2,1)}, u32[]{:S(2)}) %copy-start.2) | copy-done | bytes 524312
  4.4 0.0 copy-start.3
  4.5 1.0 %copy-done.3 = bf16[1,128,2048]{2,1,0:T(8,128)(2,1)S(1)} copy-done((bf16[1,128,2048]{2,1,0:T(8,128)(2,1)S(1)}, bf16[1,128,2048]{2,1,0:T(8,128)(2,1)}, u32[]{:S(2)}) %copy-start.3) | copy-done | bytes 524312
  5.5 65.4 %attention_exchange.1 = (bf16[1,128,2048]{2,1,0:T(8,128)(2,1)S(1)}, bf16[1,128,2048]{2,1,0:T(8,128)(2,1)S(1)}, bf16[1,128,2048]{2,1,0:T(8,128)(2,1)S(1)}, bf16[1,128,2048]{2,1,0:T(8,128)(2,1)S(1)}, f32[8,128]{1,0:T(8,128)S(1)}) custom-call(bf16[1,128,2048]{2,1,0:T(8,128)(2,1)S(1)} %copy-done, bf16[1,128,2048]{2,1,0:T(8,128)(2,1)S(1)} %copy-done.1, ...), custom_call_target="tpu_custom_call" | custom-call | tf_op jit(solution)/shard_map/attention_exchange/pallas_call | solution.py:208
  70.9 0.5 slice_bitcast_fusion
  71.5 0.8 %copy.17 = bf16[1,128,2048]{2,1,0:T(8,128)(2,1)} copy(bf16[1,128,2048]{2,1,0:T(8,128)(2,1)S(1)} %get-tuple-element.24) | data formatting | bytes 1048576
  72.2 0.8 %copy.18 = bf16[1,128,2048]{2,1,0:T(8,128)(2,1)} copy(bf16[1,128,2048]{2,1,0:T(8,128)(2,1)S(1)} %get-tuple-element.25) | data formatting | bytes 1048576
  73.0 0.8 %copy.19 = bf16[1,128,2048]{2,1,0:T(8,128)(2,1)} copy(bf16[1,128,2048]{2,1,0:T(8,128)(2,1)S(1)} %get-tuple-element.26) | data formatting | bytes 1048576
  73.8 0.8 %copy.20 = bf16[1,128,2048]{2,1,0:T(8,128)(2,1)} copy(bf16[1,128,2048]{2,1,0:T(8,128)(2,1)S(1)} %get-tuple-element.27) | data formatting | bytes 1048576
Async XLA Ops:
  0.6 0.7 copy-start.4
  0.6 0.7 copy-start.5
  0.7 0.7 copy-start.6
  1.3 1.0 %copy-start = (bf16[1,128,2048]{2,1,0:T(8,128)(2,1)S(1)}, bf16[1,128,2048]{2,1,0:T(8,128)(2,1)}, u32[]{:S(2)}) copy-start(bf16[1,128,2048]{2,1,0:T(8,128)(2,1)} %q_ref.1) | copy-start | bytes 1572868
  2.4 1.0 %copy-start.1 = (bf16[1,128,2048]{2,1,0:T(8,128)(2,1)S(1)}, bf16[1,128,2048]{2,1,0:T(8,128)(2,1)}, u32[]{:S(2)}) copy-start(bf16[1,128,2048]{2,1,0:T(8,128)(2,1)} %k_ref.1) | copy-start | bytes 1572868
  3.4 1.0 %copy-start.2 = (bf16[1,128,2048]{2,1,0:T(8,128)(2,1)S(1)}, bf16[1,128,2048]{2,1,0:T(8,128)(2,1)}, u32[]{:S(2)}) copy-start(bf16[1,128,2048]{2,1,0:T(8,128)(2,1)} %v_ref.1) | copy-start | bytes 1572868
  4.4 1.0 %copy-start.3 = (bf16[1,128,2048]{2,1,0:T(8,128)(2,1)S(1)}, bf16[1,128,2048]{2,1,0:T(8,128)(2,1)}, u32[]{:S(2)}) copy-start(bf16[1,128,2048]{2,1,0:T(8,128)(2,1)} %g_ref.1) | copy-start | bytes 1572868
where the time goes:
time: 74.9 us; the launch traced here: 74.6 us
  Pallas kernels  65.4 us (87%)
  local copies, waits for them, and re-layouts  8.52 us (11%)
    pallas_call x1, Pallas kernels, shards(): pl.pallas_call(functools.partial(kernel, sizes, heads), name='attention_e...  65.4 us
    unnamed x18, local copies, waits for them, and re-layouts  8 us

commit v1 on v0

--- a/solution.py
+++ b/solution.py
@@ -12,6 +12,7 @@
 NORM_EPSILON = 1e-06
 MESH = pl.DeviceIdType.MESH
 QROWS = 256
+HUB = 0
 NT = (((1,), (1,)), ((), ()))
 NN = (((1,), (0,)), ((), ()))
 
@@ -31,9 +32,9 @@
     return grad, jnp.sum(upstream * x * r, axis=0, keepdims=True)
 
 
-def kernel(sizes, heads, q_ref, k_ref, v_ref, g_ref, qg_ref, kg_ref, blocks_ref,
+def kernel(sizes, heads, q_ref, k_ref, v_ref, g_ref, qg_hbm, kg_hbm, blocks_hbm,
            o_ref, dq_ref, dk_ref, dv_ref, gain_ref,
-           inb, outb, keyc, keyt, valm, valt, dk_acc, dv_acc, red_a, red_b, red_c,
+           qg_ref, kg_ref, blocks_ref, small_sem, inb, outb, keyc, keyt, valm, valt, dk_acc, dv_acc, red_a, red_b, red_c, red_d, go_sem,
            in_send, in_recv, out_send, out_recv, red_send, red_recv):
     n, ny, nz = sizes
     dp = lax.axis_index("dp")
@@ -45,14 +46,14 @@
     total = rows * n
     width = qg_ref.shape[1]
 
-    barrier = pltpu.get_barrier_semaphore()
-    for d in range(1, n):
-        pl.semaphore_signal(barrier, inc=1, device_id=(dp, lax.rem(me + d, n)), device_id_type=MESH)
-    for d in range(1, ny):
-        pl.semaphore_signal(barrier, inc=1, device_id=(lax.rem(y + d, ny) * nz + z, me), device_id_type=MESH)
-    for d in range(1, nz):
-        pl.semaphore_signal(barrier, inc=1, device_id=(y * nz + lax.rem(z + d, nz), me), device_id_type=MESH)
-    pl.semaphore_wait(barrier, n + ny + nz - 3)
+    smalls = [
+        pltpu.make_async_copy(source, target, small_sem.at[i])
+        for i, (source, target) in enumerate(
+            ((qg_hbm, qg_ref), (kg_hbm, kg_ref), (blocks_hbm, blocks_ref))
+        )
+    ]
+    for copy in smalls:
+        copy.start()
 
     my_rows = pl.ds(pl.multiple_of(me * rows, rows), rows)
 
@@ -65,6 +66,36 @@
                 ins[a].at[0, :, head_columns(me, j)], inb.at[a, j, my_rows, :], in_recv.at[j, a]
             ).start()
 
+    barrier = pltpu.get_barrier_semaphore()
+
+    def greet(d, carry):
+        peer = lax.rem(me + d, n)
+
+        @pl.when(peer != HUB)
+        def _():
+            pl.semaphore_signal(barrier, inc=1, device_id=(dp, peer), device_id_type=MESH)
+
+        return carry
+
+    lax.fori_loop(1, n, greet, 0)
+
+    @pl.when(me == HUB)
+    def _():
+        for d in range(1, ny):
+            pl.semaphore_signal(barrier, inc=1, device_id=(lax.rem(y + d, ny) * nz + z, me), device_id_type=MESH)
+        for d in range(1, nz):
+            pl.semaphore_signal(barrier, inc=1, device_id=(y * nz + lax.rem(z + d, nz), me), device_id_type=MESH)
+
+    @pl.when(me != HUB)
+    def _():
+        pl.semaphore_wait(barrier, n - 1)
+        pl.semaphore_signal(go_sem, inc=1, device_id=(dp, HUB), device_id_type=MESH)
+
+    @pl.when(me == HUB)
+    def _():
+        pl.semaphore_wait(go_sem, n - 1)
+
+    for j in range(heads):
         def send(d, carry, j=j):
             peer = lax.rem(me + d, n)
             for a in range(4):
@@ -80,6 +111,8 @@
 
         lax.fori_loop(1, n, send, 0)
 
+    for copy in smalls:
+        copy.wait()
     length = blocks_ref[dp] * BLOCK
     q_gain = qg_ref[...]
     k_gain = kg_ref[...]
@@ -141,47 +174,80 @@
                 outb.at[a, j, my_rows, :], outs[a].at[0, :, head_columns(me, j)], out_recv.at[a]
             ).start()
 
-        def give(d, carry, j=j):
-            peer = lax.rem(me + d, n)
-            for a in range(4):
-                pltpu.make_async_remote_copy(
-                    src_ref=outb.at[a, j, pl.ds(pl.multiple_of(peer * rows, rows), rows), :],
-                    dst_ref=outs[a].at[0, :, head_columns(me, j)],
-                    send_sem=out_send.at[j, a],
-                    recv_sem=out_recv.at[a],
-                    device_id=(dp, peer),
-                    device_id_type=MESH,
-                ).start()
-            return carry
-
-        lax.fori_loop(1, n, give, 0)
-
-    part = jnp.concatenate([gain_q, gain_k, jnp.zeros((6, width), jnp.float32)], axis=0)
-    stages = (
-        (red_a, n, me, lambda p: (dp, p)),
-        (red_b, ny, y, lambda p: (p * nz + z, me)),
-        (red_c, nz, z, lambda p: (y * nz + p, me)),
-    )
-    for s, (slots, count, mine, place) in enumerate(stages):
-        slots[mine] = part
-        copies = []
-        for d in range(1, count):
-            copies.append(pltpu.make_async_remote_copy(
-                src_ref=slots.at[mine],
-                dst_ref=slots.at[mine],
-                send_sem=red_send.at[s, d],
-                recv_sem=red_recv.at[s, d],
-                device_id=place(lax.rem(mine + d, count)),
-                device_id_type=MESH,
-            ))
-        for copy in copies:
+        def give_back(arrays, j=j):
+            def give(d, carry):
+                peer = lax.rem(me + d, n)
+                for a in arrays:
+                    pltpu.make_async_remote_copy(
+                        src_ref=outb.at[a, j, pl.ds(pl.multiple_of(peer * rows, rows), rows), :],
+                        dst_ref=outs[a].at[0, :, head_columns(me, j)],
+                        send_sem=out_send.at[j, a],
+                        recv_sem=out_recv.at[a],
+                        device_id=(dp, peer),
+                        device_id_type=MESH,
+                    ).start()
+                return carry
+
+            lax.fori_loop(1, n, give, 0)
+
+        if j < heads - 1:
+            give_back(range(4))
+
+    def small(source, target, stage, slot, device):
+        return pltpu.make_async_remote_copy(
+            src_ref=source, dst_ref=target, send_sem=red_send.at[stage, slot], recv_sem=red_recv.at[stage, slot],
+            device_id=device, device_id_type=MESH,
+        )
+
+    def gathered(slots):
+        part = slots[0]
+        for p in range(1, slots.shape[0]):
+            part = part + slots[p]
+        return part
+
+    red_a[me] = jnp.concatenate([gain_q, gain_k, jnp.zeros((6, width), jnp.float32)], axis=0)
+
+    @pl.when(me != HUB)
+    def _():
+        up = small(red_a.at[me], red_a.at[me], 0, me, (dp, HUB))
+        up.start()
+        give_back(range(4))
+        up.wait_send()
+        small(red_d, red_d, 3, me, (dp, HUB)).wait_recv()
+
+    @pl.when(me == HUB)
+    def _():
+        give_back((0,))
+        for p in range(n):
+            if p != HUB:
+                small(red_a.at[p], red_a.at[p], 0, p, (dp, p)).wait_recv()
+        red_b[y] = gathered(red_a)
+        pl.semaphore_wait(barrier, ny + nz - 2)
+        along_y = [
+            small(red_b.at[y], red_b.at[y], 1, d, (lax.rem(y + d, ny) * nz + z, me)) for d in range(1, ny)
+        ]
+        for copy in along_y:
             copy.start()
-        for copy in copies:
+        give_back((1,))
+        for copy in along_y:
             copy.wait()
-        part = slots[0]
-        for p in range(1, count):
-            part = part + slots[p]
-    gain_ref[...] = part
+        red_c[z] = gathered(red_b)
+        along_z = [
+            small(red_c.at[z], red_c.at[z], 2, d, (y * nz + lax.rem(z + d, nz), me)) for d in range(1, nz)
+        ]
+        for copy in along_z:
+            copy.start()
+        give_back((2, 3))
+        for copy in along_z:
+            copy.wait()
+        red_d[...] = gathered(red_c)
+        down = [small(red_d, red_d, 3, p, (dp, p)) for p in range(n) if p != HUB]
+        for copy in down:
+            copy.start()
+        for copy in down:
+            copy.wait_send()
+
+    gain_ref[...] = red_d[...]
 
     for j in range(heads):
         for a in range(4):
@@ -195,23 +261,39 @@
         pltpu.make_async_copy(outs[a], outs[a], out_recv.at[a]).wait()
 
 
+def put_out(*refs):
+    sources, targets, sem = refs[:5], refs[5:11], refs[11]
+    pairs = [*zip(sources[:4], targets[:4])]
+    pairs += [(sources[4].at[i:i + 1], targets[4 + i]) for i in range(2)]
+    copies = [pltpu.make_async_copy(a, b, sem.at[i]) for i, (a, b) in enumerate(pairs)]
+    for copy in copies:
+        copy.start()
+    for copy in copies:
+        copy.wait()
+
+
 def shards(sizes, queries, keys, values, grad_out, q_gain, k_gain, clip_blocks):
     n, ny, nz = sizes
     rows, columns = queries.shape[1:]
     width = q_gain.shape[0]
     heads = columns // width // n
     total = rows * n
-    hbm = pl.BlockSpec(memory_space=pl.ANY)
+    hbm = pl.BlockSpec(memory_space=pltpu.HBM)
+    landed = pl.BlockSpec(memory_space=pl.ANY)
     vmem = pl.BlockSpec(memory_space=pltpu.VMEM)
     wide = jax.ShapeDtypeStruct(queries.shape, jnp.bfloat16)
     half, full = jnp.bfloat16, jnp.float32
     result = pl.pallas_call(
         functools.partial(kernel, sizes, heads),
         name="attention_exchange",
-        out_shape=(wide, wide, wide, wide, jax.ShapeDtypeStruct((8, width), full)),
-        in_specs=[hbm, hbm, hbm, hbm, vmem, vmem, pl.BlockSpec(memory_space=pltpu.SMEM)],
-        out_specs=(hbm, hbm, hbm, hbm, vmem),
+        out_shape=(*(pltpu.VMEM(queries.shape, half) for _ in range(4)), pltpu.VMEM((8, width), full)),
+        in_specs=[hbm] * 7,
+        out_specs=(landed, landed, landed, landed, vmem),
         scratch_shapes=[
+            pltpu.VMEM((1, width), full),
+            pltpu.VMEM((1, width), full),
+            pltpu.SMEM(clip_blocks.shape, jnp.int32),
+            pltpu.SemaphoreType.DMA((3,)),
             pltpu.VMEM((4, heads, total, width), half),
             pltpu.VMEM((4, heads, total, width), half),
             pltpu.VMEM((total, width), half),
@@ -223,19 +305,30 @@
             pltpu.VMEM((n, 8, width), full),
             pltpu.VMEM((ny, 8, width), full),
             pltpu.VMEM((nz, 8, width), full),
+            pltpu.VMEM((8, width), full),
+            pltpu.SemaphoreType.REGULAR,
             pltpu.SemaphoreType.DMA((heads, 4)),
             pltpu.SemaphoreType.DMA((heads, 4)),
             pltpu.SemaphoreType.DMA((heads, 4)),
             pltpu.SemaphoreType.DMA((4,)),
-            pltpu.SemaphoreType.DMA((3, 8)),
-            pltpu.SemaphoreType.DMA((3, 8)),
+            pltpu.SemaphoreType.DMA((4, 8)),
+            pltpu.SemaphoreType.DMA((4, 8)),
         ],
         compiler_params=pltpu.CompilerParams(
-            collective_id=0, has_side_effects=True, vmem_limit_bytes=48 * 2**20
+            collective_id=0, has_side_effects=True, vmem_limit_bytes=58 * 2**20
         ),
     )(queries, keys, values, grad_out, q_gain.reshape(1, width), k_gain.reshape(1, width), clip_blocks)
-    attended, grad_q, grad_k, grad_v, gains = result
-    return attended, grad_q, grad_k, grad_v, gains[0], gains[1]
+    gain = jax.ShapeDtypeStruct((1, width), full)
+    *tensors, gain_q, gain_k = pl.pallas_call(
+        put_out,
+        name="put_out",
+        out_shape=(wide, wide, wide, wide, gain, gain),
+        in_specs=[landed] * 5,
+        out_specs=[hbm] * 6,
+        scratch_shapes=[pltpu.SemaphoreType.DMA((6,))],
+        compiler_params=pltpu.CompilerParams(vmem_limit_bytes=8 * 2**20),
+    )(*result)
+    return *tensors, gain_q.reshape(width), gain_k.reshape(width)
 
 
 def solution(mesh):

time: 74.9 us -> 59.1 us (0.79)
  local copies, waits for them, and re-layouts: 8.52 us -> 0 us
  Pallas kernels: 65.4 us -> 58.1 us
    pallas_call x1, Pallas kernels: 65.4 us -> 56.8 us  [shards(): pl.pallas_call(functools.partial(kernel, sizes, heads), name='attention_e...]
    unnamed x18 -> x0, local copies, waits for them, and re-layouts: 8 us -> none
    pallas_call x0 -> x1, Pallas kernels: none -> 1.37 us  [shards(): pl.pallas_call(put_out, name='put_out', out_shape=(wide, wide, wide, wide...]
where the time goes in v1:
time: 59.1 us; the launch traced here: 58.8 us
  Pallas kernels  58.1 us (98%)
  between operations  0.64 us (1%)
    pallas_call x1, Pallas kernels, shards(): pl.pallas_call(functools.partial(kernel, sizes, heads), name='attention_e...  56.8 us
    pallas_call x1, Pallas kernels, shards(): pl.pallas_call(put_out, name='put_out', out_shape=(wide, wide, wide, wide...  1.37 us

profile of v1, /device:TPU:1, one launch (start us, length us, event | category | flops | bytes accessed | tf_op | source)
XLA Modules:
  0.0 58.8 jit_solution(12385622171680043877)
XLA Ops:
  0.6 56.8 %attention_exchange.1 = (bf16[1,128,2048]{2,1,0:T(8,128)(2,1)S(1)}, bf16[1,128,2048]{2,1,0:T(8,128)(2,1)S(1)}, bf16[1,128,2048]{2,1,0:T(8,128)(2,1)S(1)}, bf16[1,128,2048]{2,1,0:T(8,128)(2,1)S(1)}, f32[8,128]{1,0:T(8,128)S(1)}) custom-call(bf16[1,128,2048]{2,1,0:T(8,128)(2,1)} %q_ref.1, bf16[1,128,2048]{2,1,0:T(8,128)(2,1)} %k_ref.1, ...), custom_call_target="tpu_custom_call" | custom-call | tf_op jit(solution)/shard_map/attention_exchange/pallas_call | solution.py:286
  57.4 1.4 %put_out.1 = (bf16[1,128,2048]{2,1,0:T(8,128)(2,1)}, bf16[1,128,2048]{2,1,0:T(8,128)(2,1)}, bf16[1,128,2048]{2,1,0:T(8,128)(2,1)}, bf16[1,128,2048]{2,1,0:T(8,12...) custom-call(bf16[1,128,2048]{2,1,0:T(8,128)(2,1)S(1)} %get-tuple-element.17.refs_0_, ...), custom_call_target="tpu_custom_call" | custom-call | tf_op jit(solution)/shard_map/put_out/pallas_call | solution.py:322

commit v2 on v1

--- a/solution.py
+++ b/solution.py
@@ -11,8 +11,12 @@
 BLOCK = 128
 NORM_EPSILON = 1e-06
 MESH = pl.DeviceIdType.MESH
-QROWS = 256
-HUB = 0
+QROWS = 512
+HUB = 3
+RELEASE = {
+    "rest": (((0, 0), (0, 1)), ((0, 2), (0, 3), (1, 0), (1, 1), (1, 2), (1, 3))),
+    "hub": (((0, 0), (0, 1), (0, 2)), ((0, 3), (1, 0)), ((1, 1), (1, 2), (1, 3))),
+}
 NT = (((1,), (1,)), ((), ()))
 NN = (((1,), (0,)), ((), ()))
 
@@ -34,13 +38,13 @@
 
 def kernel(sizes, heads, q_ref, k_ref, v_ref, g_ref, qg_hbm, kg_hbm, blocks_hbm,
            o_ref, dq_ref, dk_ref, dv_ref, gain_ref,
-           qg_ref, kg_ref, blocks_ref, small_sem, inb, outb, keyc, keyt, valm, valt, dk_acc, dv_acc, red_a, red_b, red_c, red_d, go_sem,
+           qg_ref, kg_ref, blocks_ref, small_sem, inb, outb, keyc, keyt, valm, valt, q_norm, weight, out_inv, out_all, dk_acc, dv_acc, red_a, red_b, red_c, red_d, go_sem,
            in_send, in_recv, out_send, out_recv, red_send, red_recv):
     n, ny, nz = sizes
     dp = lax.axis_index("dp")
     me = lax.axis_index("seq")
     y, z = dp // nz, lax.rem(dp, nz)
-    ins = (q_ref, k_ref, g_ref, v_ref)
+    ins = (k_ref, v_ref, q_ref, g_ref)
     outs = (o_ref, dq_ref, dk_ref, dv_ref)
     rows = q_ref.shape[1]
     total = rows * n
@@ -96,9 +100,10 @@
         pl.semaphore_wait(go_sem, n - 1)
 
     for j in range(heads):
-        def send(d, carry, j=j):
-            peer = lax.rem(me + d, n)
-            for a in range(4):
+        for a in range(4):
+
+            def send(d, carry, j=j, a=a):
+                peer = lax.rem(me + d, n)
                 pltpu.make_async_remote_copy(
                     src_ref=ins[a].at[0, :, head_columns(peer, j)],
                     dst_ref=inb.at[a, j, my_rows, :],
@@ -107,9 +112,9 @@
                     device_id=(dp, peer),
                     device_id_type=MESH,
                 ).start()
-            return carry
-
-        lax.fori_loop(1, n, send, 0)
+                return carry
+
+            lax.fori_loop(1, n, send, 0)
 
     for copy in smalls:
         copy.wait()
@@ -122,47 +127,84 @@
     gain_q = jnp.zeros((1, width), jnp.float32)
     gain_k = jnp.zeros((1, width), jnp.float32)
 
+    def give_back(j, arrays):
+        def give(d, carry):
+            peer = lax.rem(me + d, n)
+            for a in arrays:
+                pltpu.make_async_remote_copy(
+                    src_ref=outb.at[a, j, pl.ds(pl.multiple_of(peer * rows, rows), rows), :],
+                    dst_ref=outs[a].at[0, :, head_columns(me, j)],
+                    send_sem=out_send.at[j, a],
+                    recv_sem=out_recv.at[a],
+                    device_id=(dp, peer),
+                    device_id_type=MESH,
+                ).start()
+            return carry
+
+        if len(arrays):
+            lax.fori_loop(1, n, give, 0)
+
+    def sent(a, j):
+        piece = inb.at[a, j, pl.ds(0, total - rows), :]
+        return pltpu.make_async_copy(piece, piece, in_send.at[j, a])
+
+    def release(who, point):
+        for j in range(heads):
+            give_back(j, tuple(a for h, a in RELEASE[who][point] if h == j))
+
+    def arrived(a, j):
+        pltpu.make_async_copy(inb.at[a, j], inb.at[a, j], in_recv.at[j, a]).wait()
+
     for j in range(heads):
-        for a in range(4):
-            pltpu.make_async_copy(inb.at[a, j], inb.at[a, j], in_recv.at[j, a]).wait()
-        k_float = inb[1, j].astype(jnp.float32)
+        arrived(0, j)
+        k_float = inb[0, j].astype(jnp.float32)
         k_normed = jnp.where(live_col, k_float * inverse_rms(k_float) * (k_gain * key_scale), 0.0)
         keyc[...] = k_normed.astype(jnp.bfloat16)
         keyt[...] = k_normed.T.astype(jnp.bfloat16)
-        v_float = jnp.where(live_col, inb[3, j].astype(jnp.float32), 0.0)
+        arrived(1, j)
+        v_float = jnp.where(live_col, inb[1, j].astype(jnp.float32), 0.0)
         valm[...] = v_float.astype(jnp.bfloat16)
         valt[0:width, :] = v_float.T.astype(jnp.bfloat16)
         live_lane = lax.broadcasted_iota(jnp.int32, (16, total), 1) < length
         valt[width:, :] = jnp.where(live_lane, 1.0, 0.0).astype(jnp.bfloat16)
-        dk_acc[...] = jnp.zeros_like(dk_acc)
-        dv_acc[...] = jnp.zeros_like(dv_acc)
-
-        def block(i, gain_q, j=j):
-            at = pl.ds(pl.multiple_of(i * QROWS, QROWS), QROWS)
-            q_float = inb[0, j, at, :].astype(jnp.float32)
-            r_q = inverse_rms(q_float)
-            q_half = (q_float * r_q * q_gain).astype(jnp.bfloat16)
-            e = jnp.exp2(dot(keyc[...], q_half, NT))
-            e_half = e.astype(jnp.bfloat16)
-            out_ext = dot(valt[...], e_half, NN)
-            live = i * QROWS + lax.broadcasted_iota(jnp.int32, (1, QROWS), 1) < length
+        arrived(2, j)
+        for at in range(0, total, QROWS):
+            q_float = inb[2, j, at:at + QROWS, :].astype(jnp.float32)
+            q_half = (q_float * inverse_rms(q_float) * q_gain).astype(jnp.bfloat16)
+            q_norm[at:at + QROWS, :] = q_half
+            e = jnp.exp2(dot(keyc[...], q_half, NT)).astype(jnp.bfloat16)
+            weight[:, at:at + QROWS] = e
+            out_ext = dot(valt[...], e, NN)
+            live = at + lax.broadcasted_iota(jnp.int32, (1, QROWS), 1) < length
             inv = jnp.where(live, 1.0 / out_ext[width:width + 1, :], 0.0)
             out_t = out_ext[0:width, :] * inv
-            g_t = inb[2, j, at, :].astype(jnp.float32).T * inv
+            out_inv[:, at:at + QROWS] = jnp.broadcast_to(inv, (8, QROWS))
+            out_all[:, at:at + QROWS] = out_t
+            outb[0, j, at:at + QROWS, :] = out_t.T.astype(jnp.bfloat16)
+
+        arrived(3, j)
+        for at in range(0, total, QROWS):
+            e = weight[:, at:at + QROWS]
+            q_half = q_norm[at:at + QROWS, :]
+            g_t = inb[3, j, at:at + QROWS, :].astype(jnp.float32).T * out_inv[0:1, at:at + QROWS]
             gs = g_t.astype(jnp.bfloat16)
-            row_dot = jnp.sum(g_t * out_t, axis=0, keepdims=True)
+            row_dot = jnp.sum(g_t * out_all[:, at:at + QROWS], axis=0, keepdims=True)
             grad_probs = dot(valm[...], gs, NN)
-            ds = (e * (grad_probs - row_dot)).astype(jnp.bfloat16)
-            dv_acc[...] += dot(e_half, gs, NT)
-            dk_acc[...] += dot(ds, q_half, NN)
+            ds = (e.astype(jnp.float32) * (grad_probs - row_dot)).astype(jnp.bfloat16)
+            add_v = dot(e, gs, NT)
+            add_k = dot(ds, q_half, NN)
+            if at == 0:
+                dv_acc[...] = add_v
+                dk_acc[...] = add_k
+            else:
+                dv_acc[...] += add_v
+                dk_acc[...] += add_k
             grad_qnorm = dot(keyt[...], ds, NN).T * math.log(2.0)
-            grad_q, part = norm_back(q_float, r_q, q_gain, grad_qnorm)
-            outb[0, j, at, :] = out_t.T.astype(jnp.bfloat16)
-            outb[1, j, at, :] = grad_q.astype(jnp.bfloat16)
-            return gain_q + part
-
-        gain_q = lax.fori_loop(0, total // QROWS, block, gain_q)
-        k_float = inb[1, j].astype(jnp.float32)
+            q_float = inb[2, j, at:at + QROWS, :].astype(jnp.float32)
+            grad_q, part = norm_back(q_float, inverse_rms(q_float), q_gain, grad_qnorm)
+            outb[1, j, at:at + QROWS, :] = grad_q.astype(jnp.bfloat16)
+            gain_q = gain_q + part
+        k_float = inb[0, j].astype(jnp.float32)
         grad_knorm = jnp.where(live_col, dk_acc[...] * scale, 0.0)
         grad_k, part = norm_back(k_float, inverse_rms(k_float), k_gain, grad_knorm)
         gain_k = gain_k + part
@@ -174,24 +216,17 @@
                 outb.at[a, j, my_rows, :], outs[a].at[0, :, head_columns(me, j)], out_recv.at[a]
             ).start()
 
-        def give_back(arrays, j=j):
-            def give(d, carry):
-                peer = lax.rem(me + d, n)
-                for a in arrays:
-                    pltpu.make_async_remote_copy(
-                        src_ref=outb.at[a, j, pl.ds(pl.multiple_of(peer * rows, rows), rows), :],
-                        dst_ref=outs[a].at[0, :, head_columns(me, j)],
-                        send_sem=out_send.at[j, a],
-                        recv_sem=out_recv.at[a],
-                        device_id=(dp, peer),
-                        device_id_type=MESH,
-                    ).start()
-                return carry
-
-            lax.fori_loop(1, n, give, 0)
-
-        if j < heads - 1:
-            give_back(range(4))
+        if j == 0:
+            for a in range(4):
+                sent(a, heads - 1).wait()
+
+            @pl.when(me != HUB)
+            def _():
+                release("rest", 0)
+
+            @pl.when(me == HUB)
+            def _():
+                release("hub", 0)
 
     def small(source, target, stage, slot, device):
         return pltpu.make_async_remote_copy(
@@ -211,13 +246,12 @@
     def _():
         up = small(red_a.at[me], red_a.at[me], 0, me, (dp, HUB))
         up.start()
-        give_back(range(4))
+        release("rest", 1)
         up.wait_send()
         small(red_d, red_d, 3, me, (dp, HUB)).wait_recv()
 
     @pl.when(me == HUB)
     def _():
-        give_back((0,))
         for p in range(n):
             if p != HUB:
                 small(red_a.at[p], red_a.at[p], 0, p, (dp, p)).wait_recv()
@@ -228,7 +262,7 @@
         ]
         for copy in along_y:
             copy.start()
-        give_back((1,))
+        release("hub", 1)
         for copy in along_y:
             copy.wait()
         red_c[z] = gathered(red_b)
@@ -237,7 +271,7 @@
         ]
         for copy in along_z:
             copy.start()
-        give_back((2, 3))
+        release("hub", 2)
         for copy in along_z:
             copy.wait()
         red_d[...] = gathered(red_c)
@@ -251,9 +285,8 @@
 
     for j in range(heads):
         for a in range(4):
-            pltpu.make_async_copy(
-                inb.at[a, j, pl.ds(0, total - rows), :], inb.at[a, j, pl.ds(0, total - rows), :], in_send.at[j, a]
-            ).wait()
+            if j < heads - 1:
+                sent(a, j).wait()
             pltpu.make_async_copy(
                 outb.at[a, j, pl.ds(0, total - rows), :], outb.at[a, j, pl.ds(0, total - rows), :], out_send.at[j, a]
             ).wait()
@@ -300,6 +333,10 @@
             pltpu.VMEM((width, total), half),
             pltpu.VMEM((total, width), half),
             pltpu.VMEM((width + 16, total), half),
+            pltpu.VMEM((total, width), half),
+            pltpu.VMEM((total, total), half),
+            pltpu.VMEM((8, total), full),
+            pltpu.VMEM((width, total), full),
             pltpu.VMEM((total, width), full),
             pltpu.VMEM((total, width), full),
             pltpu.VMEM((n, 8, width), full),

time: 59.1 us -> 55.5 us (0.939)
  Pallas kernels: 58.1 us -> 54.8 us
    pallas_call x1, Pallas kernels: 56.8 us -> 53.5 us  [shards(): pl.pallas_call(functools.partial(kernel, sizes, heads), name='attention_e...]
where the time goes in v2:
time: 55.5 us
  Pallas kernels  54.8 us (99%)
  between operations  0.64 us (1%)
    pallas_call x1, Pallas kernels, shards(): pl.pallas_call(functools.partial(kernel, sizes, heads), name='attention_e...  53.5 us
    pallas_call x1, Pallas kernels, shards(): pl.pallas_call(put_out, name='put_out', out_shape=(wide, wide, wide, wide...  1.37 us

profile of v2, /device:TPU:1, one launch (start us, length us, event | category | flops | bytes accessed | tf_op | source)
XLA Modules:
  0.0 55.5 jit_solution(4548148110541193564)
XLA Ops:
  0.6 53.5 %attention_exchange.1 = (bf16[1,128,2048]{2,1,0:T(8,128)(2,1)S(1)}, bf16[1,128,2048]{2,1,0:T(8,128)(2,1)S(1)}, bf16[1,128,2048]{2,1,0:T(8,128)(2,1)S(1)}, bf16[1,128,2048]{2,1,0:T(8,128)(2,1)S(1)}, f32[8,128]{1,0:T(8,128)S(1)}) custom-call(bf16[1,128,2048]{2,1,0:T(8,128)(2,1)} %q_ref.1, bf16[1,128,2048]{2,1,0:T(8,128)(2,1)} %k_ref.1, ...), custom_call_target="tpu_custom_call" | custom-call | tf_op jit(solution)/shard_map/attention_exchange/pallas_call | solution.py:319
  54.1 1.4 %put_out.1 = (bf16[1,128,2048]{2,1,0:T(8,128)(2,1)}, bf16[1,128,2048]{2,1,0:T(8,128)(2,1)}, bf16[1,128,2048]{2,1,0:T(8,128)(2,1)}, bf16[1,128,2048]{2,1,0:T(8,12...) custom-call(bf16[1,128,2048]{2,1,0:T(8,128)(2,1)S(1)} %get-tuple-element.17.refs_0_, ...), custom_call_target="tpu_custom_call" | custom-call | tf_op jit(solution)/shard_map/put_out/pallas_call | solution.py:359

commit v3 on v2

--- a/solution.py
+++ b/solution.py
@@ -50,6 +50,19 @@
     total = rows * n
     width = qg_ref.shape[1]
 
+    barrier = pltpu.get_barrier_semaphore()
+
+    def greet(d, carry):
+        peer = lax.rem(me + d, n)
+
+        @pl.when(peer != HUB)
+        def _():
+            pl.semaphore_signal(barrier, inc=1, device_id=(dp, peer), device_id_type=MESH)
+
+        return carry
+
+    lax.fori_loop(1, n, greet, 0)
+
     smalls = [
         pltpu.make_async_copy(source, target, small_sem.at[i])
         for i, (source, target) in enumerate(
@@ -69,26 +82,6 @@
             pltpu.make_async_copy(
                 ins[a].at[0, :, head_columns(me, j)], inb.at[a, j, my_rows, :], in_recv.at[j, a]
             ).start()
-
-    barrier = pltpu.get_barrier_semaphore()
-
-    def greet(d, carry):
-        peer = lax.rem(me + d, n)
-
-        @pl.when(peer != HUB)
-        def _():
-            pl.semaphore_signal(barrier, inc=1, device_id=(dp, peer), device_id_type=MESH)
-
-        return carry
-
-    lax.fori_loop(1, n, greet, 0)
-
-    @pl.when(me == HUB)
-    def _():
-        for d in range(1, ny):
-            pl.semaphore_signal(barrier, inc=1, device_id=(lax.rem(y + d, ny) * nz + z, me), device_id_type=MESH)
-        for d in range(1, nz):
-            pl.semaphore_signal(barrier, inc=1, device_id=(y * nz + lax.rem(z + d, nz), me), device_id_type=MESH)
 
     @pl.when(me != HUB)
     def _():
@@ -115,6 +108,13 @@
                 return carry
 
             lax.fori_loop(1, n, send, 0)
+
+    @pl.when(me == HUB)
+    def _():
+        for d in range(1, ny):
+            pl.semaphore_signal(barrier, inc=1, device_id=(lax.rem(y + d, ny) * nz + z, me), device_id_type=MESH)
+        for d in range(1, nz):
+            pl.semaphore_signal(barrier, inc=1, device_id=(y * nz + lax.rem(z + d, nz), me), device_id_type=MESH)
 
     for copy in smalls:
         copy.wait()

time: 55.5 us -> 55.5 us (level)
  no operation moved by 1% of the time
where the time goes in v3:
time: 55.5 us
  Pallas kernels  54.8 us (99%)
  between operations  0.64 us (1%)
    pallas_call x1, Pallas kernels, shards(): pl.pallas_call(functools.partial(kernel, sizes, heads), name='attention_e...  53.4 us
    pallas_call x1, Pallas kernels, shards(): pl.pallas_call(put_out, name='put_out', out_shape=(wide, wide, wide, wide...  1.37 us

profile of v3, /device:TPU:1, one launch (start us, length us, event | category | flops | bytes accessed | tf_op | source)
XLA Modules:
  0.0 55.5 jit_solution(13091278187480160201)
XLA Ops:
  0.6 53.4 %attention_exchange.1 = (bf16[1,128,2048]{2,1,0:T(8,128)(2,1)S(1)}, bf16[1,128,2048]{2,1,0:T(8,128)(2,1)S(1)}, bf16[1,128,2048]{2,1,0:T(8,128)(2,1)S(1)}, bf16[1,128,2048]{2,1,0:T(8,128)(2,1)S(1)}, f32[8,128]{1,0:T(8,128)S(1)}) custom-call(bf16[1,128,2048]{2,1,0:T(8,128)(2,1)} %q_ref.1, bf16[1,128,2048]{2,1,0:T(8,128)(2,1)} %k_ref.1, ...), custom_call_target="tpu_custom_call" | custom-call | tf_op jit(solution)/shard_map/attention_exchange/pallas_call | solution.py:319
  54.1 1.4 %put_out.1 = (bf16[1,128,2048]{2,1,0:T(8,128)(2,1)}, bf16[1,128,2048]{2,1,0:T(8,128)(2,1)}, bf16[1,128,2048]{2,1,0:T(8,128)(2,1)}, bf16[1,128,2048]{2,1,0:T(8,12...) custom-call(bf16[1,128,2048]{2,1,0:T(8,128)(2,1)S(1)} %get-tuple-element.17.refs_0_, ...), custom_call_target="tpu_custom_call" | custom-call | tf_op jit(solution)/shard_map/put_out/pallas_call | solution.py:359

commit v4 on v3

--- a/solution.py
+++ b/solution.py
@@ -160,11 +160,10 @@
         k_float = inb[0, j].astype(jnp.float32)
         k_normed = jnp.where(live_col, k_float * inverse_rms(k_float) * (k_gain * key_scale), 0.0)
         keyc[...] = k_normed.astype(jnp.bfloat16)
-        keyt[...] = k_normed.T.astype(jnp.bfloat16)
+        keyt[...] = keyc[...].T
         arrived(1, j)
-        v_float = jnp.where(live_col, inb[1, j].astype(jnp.float32), 0.0)
-        valm[...] = v_float.astype(jnp.bfloat16)
-        valt[0:width, :] = v_float.T.astype(jnp.bfloat16)
+        valm[...] = jnp.where(live_col, inb[1, j].astype(jnp.float32), 0.0).astype(jnp.bfloat16)
+        valt[0:width, :] = valm[...].T
         live_lane = lax.broadcasted_iota(jnp.int32, (16, total), 1) < length
         valt[width:, :] = jnp.where(live_lane, 1.0, 0.0).astype(jnp.bfloat16)
         arrived(2, j)
@@ -186,7 +185,7 @@
         for at in range(0, total, QROWS):
             e = weight[:, at:at + QROWS]
             q_half = q_norm[at:at + QROWS, :]
-            g_t = inb[3, j, at:at + QROWS, :].astype(jnp.float32).T * out_inv[0:1, at:at + QROWS]
+            g_t = inb[3, j, at:at + QROWS, :].T.astype(jnp.float32) * out_inv[0:1, at:at + QROWS]
             gs = g_t.astype(jnp.bfloat16)
             row_dot = jnp.sum(g_t * out_all[:, at:at + QROWS], axis=0, keepdims=True)
             grad_probs = dot(valm[...], gs, NN)

time: 55.5 us -> 55.5 us (level)
  no operation moved by 1% of the time
where the time goes in v4:
time: 55.5 us
  Pallas kernels  54.8 us (99%)
  between operations  0.64 us (1%)
    pallas_call x1, Pallas kernels, shards(): pl.pallas_call(functools.partial(kernel, sizes, heads), name='attention_e...  53.4 us
    pallas_call x1, Pallas kernels, shards(): pl.pallas_call(put_out, name='put_out', out_shape=(wide, wide, wide, wide...  1.37 us

profile of v4, /device:TPU:1, one launch (start us, length us, event | category | flops | bytes accessed | tf_op | source)
XLA Modules:
  0.0 55.5 jit_solution(9954750509079728031)
XLA Ops:
  0.6 53.4 %attention_exchange.1 = (bf16[1,128,2048]{2,1,0:T(8,128)(2,1)S(1)}, bf16[1,128,2048]{2,1,0:T(8,128)(2,1)S(1)}, bf16[1,128,2048]{2,1,0:T(8,128)(2,1)S(1)}, bf16[1,128,2048]{2,1,0:T(8,128)(2,1)S(1)}, f32[8,128]{1,0:T(8,128)S(1)}) custom-call(bf16[1,128,2048]{2,1,0:T(8,128)(2,1)} %q_ref.1, bf16[1,128,2048]{2,1,0:T(8,128)(2,1)} %k_ref.1, ...), custom_call_target="tpu_custom_call" | custom-call | tf_op jit(solution)/shard_map/attention_exchange/pallas_call | solution.py:318
  54.1 1.4 %put_out.1 = (bf16[1,128,2048]{2,1,0:T(8,128)(2,1)}, bf16[1,128,2048]{2,1,0:T(8,128)(2,1)}, bf16[1,128,2048]{2,1,0:T(8,128)(2,1)}, bf16[1,128,2048]{2,1,0:T(8,12...) custom-call(bf16[1,128,2048]{2,1,0:T(8,128)(2,1)S(1)} %get-tuple-element.17.refs_0_, ...), custom_call_target="tpu_custom_call" | custom-call | tf_op jit(solution)/shard_map/put_out/pallas_call | solution.py:358
